TPU v7x, 32 devices: a whole 2x2x4 slice. The times are simulated.
32 devices in a mesh: tm: 4 (over x, core), space: 8 (over z, y).
Axes of the slice: x: 2, y: 2, z: 4, core: 2. Of those that a mesh axis runs over, the one named last changes fastest.
Arguments:
- pixels: bfloat16 [163840, 128], P(('tm', 'space')), may hold values from -48 to 48
- weights: bfloat16 [163840], P(('tm', 'space')), may hold values from 0.5 to 2
- tile_index: int32 [163840], P(('tm', 'space')), may hold values from 0 to 7, as said below
- tile_row: int32 [163840], P(('tm', 'space')), may hold values from 0 to 159, as said below
- granule_day: int32 [163840], P(('tm', 'space')), may hold values from 0 to 127
Outputs:
- field: bfloat16 [8, 160, 512, 128], P('space', 'tm')
- basis: bfloat16 [8, 160, 256, 128], P('space', 'tm')
- propagator: float32 [256, 256], replicated
Inputs may be any that keep to these rules, and one draw needn't show every extreme that they name: `tile_index`: of the rows of one device, at most 1280 name one tile, and in every device's rows some tile is named by exactly 1280. `tile_row`: of the rows of one device, at most 320 name one tile and a grid row from k * 40 to (k + 1) * 40 - 1 for one k, and in every device's rows some tile and k reach 320.
All inputs are finite; a program needn't handle non-finite values.
Results may differ from a plain program's by a relative error of at most 0.0061.
Values may be sent and summed in bfloat16 or wider, within the bound.
No kernel may reach another device: no remote copies, remote signals or barrier semaphores. Data moves between devices by JAX's collectives and lax.ppermute only.
A program may use at most 64 MiB of HBM per device.

v0:
```python
import math

import jax
import jax.numpy as jnp
from jax import lax
from jax.sharding import PartitionSpec as P

GR_DEV = 160
DAYS = 512
RANK = 256
ITERS = 8


def bucket_slots(target_dest, dest_count, slot_count):
    labels = jnp.arange(dest_count, dtype=jnp.int32)
    onehot = (target_dest[:, None] == labels[None, :]).astype(jnp.int32)
    before = jnp.cumsum(onehot, axis=0) - onehot
    rank_of = jnp.sum(before * onehot, axis=1)
    return target_dest * slot_count + rank_of


def pack_rows(pixels, weights, targets, position, dest_count, slot_count):
    size = dest_count * slot_count
    pixel_buf = jnp.zeros((size, pixels.shape[1]), pixels.dtype).at[position].set(pixels)
    weight_buf = jnp.zeros((size,), weights.dtype).at[position].set(weights)
    target_buf = jnp.zeros((size,), jnp.int32).at[position].set(targets)
    return (
        pixel_buf.reshape(dest_count, slot_count, pixels.shape[1]),
        weight_buf.reshape(dest_count, slot_count),
        target_buf.reshape(dest_count, slot_count),
    )


def grid_rows(pixel_buf, weight_buf, target_buf, cell_count):
    width = pixel_buf.shape[-1]
    flat_pixels = pixel_buf.reshape(-1, width)
    contrib = weight_buf.reshape(-1)[:, None].astype(jnp.float32) * flat_pixels.astype(jnp.float32)
    return jnp.zeros((cell_count, width), jnp.float32).at[target_buf.reshape(-1)].add(contrib)


def body(pixels, weights, tile_index, tile_row, granule_day):
    swath_rows = pixels.shape[0]
    width = pixels.shape[1]
    space_count = lax.axis_size("space")
    time_count = lax.axis_size("tm")
    day_dev = DAYS // time_count
    rows_tm = GR_DEV // time_count
    capacity = 2 * swath_rows // space_count
    my_time = lax.axis_index("tm")
    group = tile_row // rows_tm
    dest = group * space_count + tile_index
    slot_count = capacity // time_count
    targets = (tile_row - group * rows_tm) * DAYS + my_time * day_dev + granule_day
    position = bucket_slots(dest, time_count * space_count, slot_count)
    packed = pack_rows(pixels, weights, targets, position, time_count * space_count, slot_count)
    moved = (
        lax.all_to_all(packed[0], ("tm", "space"), split_axis=0, concat_axis=0, tiled=True),
        lax.all_to_all(packed[1], ("tm", "space"), split_axis=0, concat_axis=0, tiled=True),
        lax.all_to_all(packed[2], ("tm", "space"), split_axis=0, concat_axis=0, tiled=True),
    )
    gridded = grid_rows(moved[0], moved[1], moved[2], rows_tm * DAYS)
    local = gridded.astype(jnp.bfloat16).reshape(rows_tm, DAYS, width)
    partial_gram = jnp.einsum("rdp,rep->de", local, local, preferred_element_type=jnp.float32)
    gram = lax.psum(partial_gram, ("tm", "space"))
    lower = jnp.linalg.cholesky(gram)
    factor = lower.T
    cross = jnp.dot(factor[:RANK, 1:], factor[:RANK, :-1].T, precision=lax.Precision.HIGHEST)
    polar = cross / jnp.sqrt(jnp.sum(cross * cross) + 1e-06)
    for sweep in range(ITERS):
        square = jnp.dot(polar.T, polar, precision=lax.Precision.HIGHEST)
        polar = 1.5 * polar - 0.5 * jnp.dot(polar, square, precision=lax.Precision.HIGHEST)
    propagator = jnp.sqrt(jnp.float32(RANK)) * polar
    identity = jnp.eye(RANK, dtype=jnp.float32)
    inverse = jax.scipy.linalg.solve_triangular(lower[:RANK, :RANK], identity, lower=True).T
    cell_total = space_count * GR_DEV * width
    scaled_inverse = (math.sqrt(cell_total) * inverse).astype(jnp.bfloat16)
    basis = jnp.einsum(
        "rdp,dk->rkp", local[:, :RANK, :], scaled_inverse, preferred_element_type=jnp.float32
    ).astype(jnp.bfloat16)
    return (local[None], basis[None], propagator)


def solution(mesh):
    placed = (
        P(("tm", "space"), None),
        P(("tm", "space")),
        P(("tm", "space")),
        P(("tm", "space")),
        P(("tm", "space")),
    )
    return jax.shard_map(
        body,
        mesh=mesh,
        in_specs=placed,
        out_specs=(P("space", "tm", None, None), P("space", "tm", None, None), P()),
        check_vma=False,
    )
```

profile of v0, /device:TPU:0, one launch (start us, length us, event | category | flops | bytes accessed | tf_op | source)
XLA Modules:
  0.0 526.7 jit_solution(1234506629783124022)
XLA Ops:
  7.2 0.8 add_add_fusion
  8.0 9.3 %reduce-window.6 = s32[32,40,128]{2,1,0:T(8,128)S(1)} reduce-window(s32[32,40,128]{2,1,0:T(8,128)S(1)} %fusion.22, s32[]{:T(128)} %copy.35), window={size=1x1x128 pad=0_0x0_0x127_0}, to_apply=%region_0.1 | reduce-window | flops 20807680 | bytes 1310724 | tf_op jit(solution)/shard_map/reduce-window
  17.4 0.8 slice_reduce_fusion
  18.8 35.8 %scatter_custom_fusion.1 = bf16[10240]{0:T(1024)(128)(2,1)S(1)} fusion(s32[5120]{0:T(1024)S(1)} %compare_select_fusion.1, bf16[5120]{0:T(1024)(128)(2,1)} %param.6, bf16[]{:T(256)} %constant.184.clone.1), kind=kCustom, calls=%fused_computation.102 | custom fusion | bytes 20992 | tf_op jit(solution)/shard_map/scatter | solution.py:25
  54.7 0.5 broadcast.277
  55.2 0.8 reduce.29
  56.0 0.7 reshape.187
  56.7 7.3 %all-to-all-start.1 = ((bf16[32,2,160]{2,1,0:T(2,128)(2,1)}), bf16[32,2,160]{2,1,0:T(2,128)(2,1)S(1)}, u32[]{:S(2)}, u32[]{:S(2)}) async-start(bf16[32,2,160]{2,1,0:T(2,128)(2,1)} %reshape.187), calls=%async_computation.1 | async-start | bytes 65536 | tf_op jit(solution)/shard_map/all_to_all | solution.py:58
  64.0 19.3 %scatter_custom_fusion = s32[10240]{0:T(1024)S(1)} fusion(s32[5120]{0:T(1024)S(1)} %compare_select_fusion.1, s32[5120]{0:T(1024)S(1)} %get-tuple-element.31, s32[]{:T(128)} %copy.35), kind=kCustom, calls=%fused_computation.99 | custom fusion | bytes 40964 | tf_op jit(solution)/shard_map/scatter | solution.py:26
  83.3 0.7 all_to_all.15
  84.0 5.8 %all-to-all-start = ((s32[32,1,320]{2,1,0:T(1,128)}), s32[32,1,320]{2,1,0:T(1,128)S(1)}, u32[]{:S(2)}, u32[]{:S(2)}) async-start(s32[32,1,320]{2,1,0:T(1,128)} %all_to_all.15), calls=%async_computation | async-start | bytes 98304 | tf_op jit(solution)/shard_map/all_to_all | solution.py:59
  89.8 15.6 %scatter_custom_fusion.2 = bf16[10240,128]{1,0:T(8,128)(2,1)} fusion(s32[5120]{0:T(1024)S(1)} %compare_select_fusion.1, bf16[5120,128]{1,0:T(8,128)(2,1)} %param.5, bf16[]{:T(256)} %constant.184.clone.1), kind=kCustom, calls=%fused_computation.14 | custom fusion | bytes 2621952 | tf_op jit(solution)/shard_map/scatter | solution.py:24
  105.4 5.8 %all-to-all-start.2 = ((bf16[32,320,128]{2,1,0:T(8,128)(2,1)}), bf16[32,320,128]{2,1,0:T(8,128)(2,1)S(1)}, u32[]{:S(2)}, u32[]{:S(2)}) async-start(bf16[32,320,128]{2,1,0:T(8,128)(2,1)} %bitcast.3), calls=%async_computation.2 | async-start | bytes 5242880 | tf_op jit(solution)/shard_map/all_to_all | solution.py:57
  111.3 0.3 all-reduce.3.cloned.1.call-start
  112.2 60.7 %all-to-all-done.2 = bf16[32,320,128]{2,1,0:T(8,128)(2,1)S(1)} async-done(((bf16[32,320,128]{2,1,0:T(8,128)(2,1)}), bf16[32,320,128]{2,1,0:T(8,128)(2,1)S(1)}, u32[]{:S(2)}, u32[]{:S(2)}) %all-to-all-start.2) | async-done | bytes 2621472 | tf_op jit(solution)/shard_map/all_to_all | solution.py:57
  172.9 72.8 %scatter_custom_fusion.3 = f32[20480,128]{1,0:T(8,128)} fusion(s32[10240]{0:T(1024)S(1)} %bitcast.114, bf16[10240,128]{1,0:T(8,128)(2,1)S(1)} %bitcast.110, f32[]{:T(128)} %constant.172.clone.1, f32[10240]{0:T(1024)S(1)} %reshape.137), kind=kCustom, calls=%fused_computation.7 | custom fusion | flops 3932160 | bytes 13148164 | tf_op jit(solution)/shard_map/scatter-add | solution.py:38
  245.7 4.6 convert_element_type.44
  250.3 2.3 copy-done
  252.6 3.9 convolution_bitcast_fusion
  256.6 127.5 %all-reduce.3.cloned.1.call-done = f32[512,512]{0,1:T(8,128)} async-done(((f32[512,512]{0,1:T(8,128)}), f32[512,512]{0,1:T(8,128)}) %all-reduce.3.cloned.1.call-update) | async-done | bytes 1048592 | tf_op jit(solution)/shard_map/psum | solution.py:64
  384.1 1.6 copy.14
  385.6 1.4 fusion.18
  387.1 11.7 %cholesky.104 = f32[128,128]{1,0:T(8,128)S(1)} custom-call(f32[128,128]{1,0:T(8,128)S(1)} %cholesky.266), custom_call_target="Cholesky" | custom-call | tf_op jit(solution)/shard_map/jit(cholesky)/cholesky | solution.py:65
  399.0 9.8 %custom-call.31 = f32[1,128,128]{1,2,0:T(8,128)S(1)} custom-call(f32[1,128,128]{2,1,0:T(8,128)S(1)} %get-tuple-element.30), custom_call_target="InvertDiagBlocksLowerTriangular" | custom-call | tf_op jit(solution)/shard_map/jit(cholesky)/cholesky | solution.py:65
  408.8 0.3 constant_dynamic-update-slice_fusion.3
  409.1 0.3 convolution_subtract_fusion
  409.5 20.4 %cholesky.217 = f32[128,128]{1,0:T(8,128)S(1)} custom-call(f32[128,128]{1,0:T(8,128)S(1)} %cholesky.270), custom_call_target="Cholesky" | custom-call | tf_op jit(solution)/shard_map/jit(cholesky)/cholesky | solution.py:65
  429.9 9.8 %custom-call.32 = f32[1,128,128]{1,2,0:T(8,128)S(1)} custom-call(f32[1,128,128]{2,1,0:T(8,128)S(1)} %get-tuple-element.27), custom_call_target="InvertDiagBlocksLowerTriangular" | custom-call | tf_op jit(solution)/shard_map/jit(cholesky)/cholesky | solution.py:65
  439.7 0.3 convolution_dynamic-update-slice_fusion
  440.0 0.4 convolution_subtract_fusion.1
  440.4 11.7 %cholesky.238 = f32[128,128]{1,0:T(8,128)S(1)} custom-call(f32[128,128]{1,0:T(8,128)S(1)} %cholesky.275), custom_call_target="Cholesky" | custom-call | tf_op jit(solution)/shard_map/jit(cholesky)/cholesky | solution.py:65
  452.2 0.7 compare_reduce_fusion.1
  452.9 9.8 %custom-call.33 = f32[1,128,128]{1,2,0:T(8,128)S(1)} custom-call(f32[1,128,128]{2,1,0:T(8,128)S(1)} %get-tuple-element.24), custom_call_target="InvertDiagBlocksLowerTriangular" | custom-call | tf_op jit(solution)/shard_map/jit(cholesky)/cholesky | solution.py:65
  462.9 0.4 convolution_subtract_fusion.3
  463.3 11.9 %cholesky.255 = f32[128,128]{1,0:T(8,128)S(1)} custom-call(f32[128,128]{1,0:T(8,128)S(1)} %convolution_subtract_fusion.3), custom_call_target="Cholesky" | custom-call | tf_op jit(solution)/shard_map/jit(cholesky)/cholesky | solution.py:65
  475.2 0.6 compare_reduce_fusion
  475.9 0.6 compare_reduce_fusion.2
  479.3 1.6 multiply_reduce_fusion
  481.6 0.6 fusion.38
  482.3 0.4 fusion.16
  482.6 0.6 fusion.54
  483.2 0.4 fusion.15
  483.6 0.6 fusion.55
  484.2 0.4 fusion.14
  484.6 0.6 fusion.56
  485.2 0.4 fusion.13
  485.6 0.6 fusion.57
  486.2 0.4 fusion.12
  486.6 0.6 fusion.58
  487.2 0.4 fusion.11
  487.6 0.6 fusion.59
  488.2 0.4 fusion.10
  488.6 0.6 fusion.60
  489.2 1.1 fusion.17
  490.4 4.1 while.1
  490.4 0.6 fusion.97
  491.0 1.4 bitcast_dynamic-update-slice_fusion.2
  492.4 0.6 fusion.97
  493.0 1.4 bitcast_dynamic-update-slice_fusion.2
  494.5 19.9 %custom-call.34 = f32[2,128,128]{1,2,0:T(8,128)S(1)} custom-call(f32[2,128,128]{2,1,0:T(8,128)S(1)} %get-tuple-element.10), custom_call_target="InvertDiagBlocksLowerTriangular" | custom-call | tf_op jit(solution)/shard_map/jit(_solve_triangular)/triangular_solve | solution.py:74
  514.4 0.3 fusion.36
  514.7 0.3 convolution_subtract_fusion.2
  514.9 0.3 fusion.40
  515.3 4.1 convert_bitcast_fusion
  (34 shorter events, 2.3 us)
Async XLA Ops:
  56.7 27.3 %all-to-all-start.1 = ((bf16[32,2,160]{2,1,0:T(2,128)(2,1)}), bf16[32,2,160]{2,1,0:T(2,128)(2,1)S(1)}, u32[]{:S(2)}, u32[]{:S(2)}) async-start(bf16[32,2,160]{2,1,0:T(2,128)(2,1)} %reshape.187), calls=%async_computation.1 | async-start | bytes 65536 | tf_op jit(solution)/shard_map/all_to_all | solution.py:58
  84.0 21.4 %all-to-all-start = ((s32[32,1,320]{2,1,0:T(1,128)}), s32[32,1,320]{2,1,0:T(1,128)S(1)}, u32[]{:S(2)}, u32[]{:S(2)}) async-start(s32[32,1,320]{2,1,0:T(1,128)} %all_to_all.15), calls=%async_computation | async-start | bytes 98304 | tf_op jit(solution)/shard_map/all_to_all | solution.py:59
  105.4 67.5 %all-to-all-start.2 = ((bf16[32,320,128]{2,1,0:T(8,128)(2,1)}), bf16[32,320,128]{2,1,0:T(8,128)(2,1)S(1)}, u32[]{:S(2)}, u32[]{:S(2)}) async-start(bf16[32,320,128]{2,1,0:T(8,128)(2,1)} %bitcast.3), calls=%async_computation.2 | async-start | bytes 5242880 | tf_op jit(solution)/shard_map/all_to_all | solution.py:57
  111.3 272.8 %all-reduce.3.cloned.1.call-start = ((), (), s32[]{:S(2)}) async-start(), calls=%async_computation.3 | async-start | bytes 2097152 | tf_op jit(solution)/shard_map/psum | solution.py:64
  250.3 2.4 copy-start
Sparse Core Ops, SparseCore 0:
  256.6 127.3 all-reduce.2
where the time goes:
time: 535 us; the launch traced here: 527 us
  other arithmetic  198 us (37%)
  waiting for transfers between devices  188 us (35%)
  local copies, waits for them, and re-layouts  81.9 us (15%)
  matrix products  20.8 us (4%)
  starting transfers between devices  19.3 us (4%)
  between operations  18.2 us (3%)
    psum x1, waiting for transfers between devices, body(): gram = lax.psum(partial_gram, ('tm', 'space'))  127 us
    another operation x14, other arithmetic, body(): lower = jnp.linalg.cholesky(gram)  87.3 us
    scatter-add x1, other arithmetic, grid_rows(): jnp.zeros((cell_count, width), jnp.float32).at[target_buf.reshape(-1)]  72.8 us
    all_to_all x1, waiting for transfers between devices, body(): lax.all_to_all(packed[0], ('tm', 'space'), split_axis=0, concat_axis=0, t...  60.7 us
    scatter x1, local copies, waits for them, and re-layouts, pack_rows(): weight_buf = jnp.zeros((size,), weights.dtype).at[position].set(weights)  35.8 us
    another operation x3, other arithmetic, body(): jax.scipy.linalg.solve_triangular(lower[:RANK, :RANK], identity, lower=True)  19.9 us
    scatter x1, local copies, waits for them, and re-layouts, pack_rows(): target_buf = jnp.zeros((size,), jnp.int32).at[position].set(targets)  19.3 us
    scatter x1, local copies, waits for them, and re-layouts, pack_rows(): jnp.zeros((size, pixels.shape[1]), pixels.dtype).at[position].set(pixels)  15.6 us
  transfers between devices with their start and end apart: 4, of which 2 were waited for; matrix products, arithmetic and copies ran while one was open for 7% of the time, Pallas kernels for 0%

commit v1 on v0

v1 whole, which is shorter than its diff:
```python
import functools
import math

import jax
import jax.numpy as jnp
from jax import lax
from jax.experimental import pallas as pl
from jax.experimental.pallas import tpu as pltpu
from jax.sharding import PartitionSpec as P

GR_DEV = 160
DAYS = 512
RANK = 256
ITERS = 8
LANES = 128
META_ROWS = 16
GRID_STEPS = 5
VMEM = 56 * 1024 * 1024

LAST_LAST = (((1,), (1,)), ((), ()))
FIRST_FIRST = (((0,), (0,)), ((), ()))


def round_up(value, unit):
    return -(-value // unit) * unit


def pack_kernel(dims, tile_ref, row_ref, day_ref, weight_ref, pix_ref, out_ref, pos_v, pos_s, pixf, outf, mrow, sem):
    time_count, space_count, rows_tm, slot_rows, width = dims
    dest_count = time_count * space_count
    chunks = tile_ref.shape[0]
    pieces = width // LANES

    tile = tile_ref[...]
    row = row_ref[...]
    group = jnp.zeros_like(row)
    for k in range(1, time_count):
        group = group + jnp.where(row >= k * rows_tm, 1, 0)
    dest_all = group * space_count + tile
    local_row = (row - group * rows_tm).astype(jnp.float32)
    day = day_ref[...].astype(jnp.float32)
    weight = weight_ref[...].astype(jnp.float32)

    dest_iota = lax.broadcasted_iota(jnp.int32, (dest_count, LANES), 0)
    slot_iota = lax.broadcasted_iota(jnp.int32, (width, LANES), 0)
    upper = jnp.where(
        lax.broadcasted_iota(jnp.int32, (LANES, LANES), 0) <= lax.broadcasted_iota(jnp.int32, (LANES, LANES), 1), 1.0, 0.0
    ).astype(jnp.bfloat16)
    carry = jnp.zeros((dest_count, 1), jnp.float32)
    meta = jnp.zeros((3 * dest_count, width), jnp.float32)
    for c in range(chunks):
        dest = dest_all[c : c + 1, :]
        hot = dest_iota == dest
        prefix = jnp.dot(jnp.where(hot, 1.0, 0.0).astype(jnp.bfloat16), upper, preferred_element_type=jnp.float32)
        rank = jnp.sum(jnp.where(hot, prefix + carry, 0.0), axis=0, keepdims=True).astype(jnp.int32) - 1
        carry = carry + prefix[:, LANES - 1 : LANES]
        pos_v[c : c + 1, :] = dest * slot_rows + rank
        place = jnp.where(slot_iota == rank, 1.0, 0.0).astype(jnp.bfloat16)
        values = jnp.concatenate(
            [jnp.where(hot, v[c : c + 1, :], 0.0) for v in (weight, local_row, day)], axis=0
        ).astype(jnp.bfloat16)
        meta = meta + lax.dot_general(values, place, LAST_LAST, preferred_element_type=jnp.float32)
    copy = pltpu.make_async_copy(pos_v, pos_s, sem)
    copy.start()

    mrow[...] = jnp.zeros_like(mrow)
    for v in range(3):
        for i in range(pieces):
            mrow[pl.ds(v * pieces + i, dest_count, stride=META_ROWS), :] = meta[
                v * dest_count : (v + 1) * dest_count, i * LANES : (i + 1) * LANES
            ]

    def widen(c, _):
        at = pl.ds(pl.multiple_of(c * LANES, LANES), LANES)
        pixf[at, :] = pix_ref[at, :].astype(jnp.float32)
        return 0

    lax.fori_loop(0, chunks, widen, 0)

    def clear(b, _):
        outf[pl.ds(pl.multiple_of(b * slot_rows, 16), slot_rows), :] = jnp.zeros((slot_rows, LANES), jnp.float32)
        return 0

    lax.fori_loop(0, dest_count, clear, 0)
    copy.wait()

    def move(c, _):
        base = c * LANES
        for lane in range(LANES):
            outf[pl.ds(pos_s[c, lane], 1), :] = pixf[pl.ds(base + lane, 1), :]
        return 0

    lax.fori_loop(0, chunks, move, 0)

    def narrow(b, _):
        out_ref[b, :slot_rows, :] = outf[pl.ds(pl.multiple_of(b * slot_rows, 16), slot_rows), :].astype(jnp.bfloat16)
        out_ref[b, slot_rows:, :] = mrow[pl.ds(pl.multiple_of(b * META_ROWS, 16), META_ROWS), :].astype(jnp.bfloat16)
        return 0

    lax.fori_loop(0, dest_count, narrow, 0)


def pack(pixels, weights, tile_index, tile_row, granule_day, time_count, space_count, rows_tm, slots):
    swath_rows = pixels.shape[0]
    chunks = swath_rows // LANES
    dest_count = time_count * space_count
    slot_rows = round_up(slots, 16)
    width = round_up(slots, LANES)
    shape = (chunks, LANES)
    return pl.pallas_call(
        functools.partial(pack_kernel, (time_count, space_count, rows_tm, slot_rows, width)),
        out_shape=jax.ShapeDtypeStruct((dest_count, slot_rows + META_ROWS, LANES), jnp.bfloat16),
        scratch_shapes=[
            pltpu.VMEM(shape, jnp.int32),
            pltpu.SMEM(shape, jnp.int32),
            pltpu.VMEM((swath_rows, LANES), jnp.float32),
            pltpu.VMEM((dest_count * slot_rows, LANES), jnp.float32),
            pltpu.VMEM((dest_count * META_ROWS, LANES), jnp.float32),
            pltpu.SemaphoreType.DMA,
        ],
        compiler_params=pltpu.CompilerParams(vmem_limit_bytes=VMEM),
        name="pack",
    )(
        tile_index.reshape(shape),
        tile_row.reshape(shape),
        granule_day.reshape(shape),
        weights.reshape(shape),
        pixels,
    )


def grid_kernel(dims, moved_ref, field_ref, gram_ref, pix2, onehot, pair_of):
    time_count, space_count, rows_tm, slot_rows, width = dims
    day_dev = DAYS // time_count
    pieces = width // LANES
    pairs = rows_tm // 2 // GRID_STEPS
    step = pl.program_id(0)

    @pl.when(step == 0)
    def _():
        gram_ref[...] = jnp.zeros_like(gram_ref)
        day_iota = lax.broadcasted_iota(jnp.int32, (day_dev, width), 0).astype(jnp.float32)

        def spread(b, _):
            m = b // space_count
            at = pl.ds(pl.multiple_of((b % space_count) * width, LANES), width)
            meta = moved_ref[b, slot_rows:, :].astype(jnp.float32)
            weight, local_row, day = (
                jnp.concatenate([meta[v * pieces + i : v * pieces + i + 1, :] for i in range(pieces)], axis=1)
                for v in range(3)
            )
            onehot[m, :, at] = jnp.where(day_iota == day, weight, 0.0).astype(jnp.bfloat16)
            half = jnp.floor(local_row * 0.5)
            pair_of[m, :, at] = jnp.broadcast_to(half, (8, width))
            odd = jnp.transpose(jnp.broadcast_to(local_row - 2.0 * half, (8, width)))[:slot_rows, 0:1]
            odd = jnp.broadcast_to(odd, (slot_rows, LANES)).astype(jnp.bfloat16)
            pix = moved_ref[b, :slot_rows, :]
            right = pix * odd
            rows = pl.ds(pl.multiple_of((b % space_count) * width, LANES), slot_rows)
            pix2[m, rows, :LANES] = pix - right
            pix2[m, rows, LANES:] = right
            if width > slot_rows:
                rest = pl.ds(pl.multiple_of((b % space_count) * width + slot_rows, 16), width - slot_rows)
                pix2[m, rest, :] = jnp.zeros((width - slot_rows, 2 * LANES), jnp.bfloat16)
            return 0

        lax.fori_loop(0, time_count * space_count, spread, 0)

    for m in range(time_count):
        mine = pair_of[m, 0:1, :]
        chosen = onehot[m]
        left = jnp.concatenate(
            [
                chosen * jnp.where(mine == (step * pairs + q).astype(jnp.float32), 1.0, 0.0).astype(jnp.bfloat16)
                for q in range(pairs)
            ],
            axis=0,
        )
        sums = jnp.dot(left, pix2[m], preferred_element_type=jnp.float32).astype(jnp.bfloat16)
        for q in range(pairs):
            here = sums[q * day_dev : (q + 1) * day_dev, :]
            field_ref[2 * q, m * day_dev : (m + 1) * day_dev, :] = here[:, :LANES]
            field_ref[2 * q + 1, m * day_dev : (m + 1) * day_dev, :] = here[:, LANES:]
    for q in range(pairs):
        both = jnp.concatenate([field_ref[2 * q], field_ref[2 * q + 1]], axis=1)
        part = lax.dot_general(both[:RANK], both, LAST_LAST, preferred_element_type=jnp.float32)
        for i in range(DAYS // LANES):
            gram_ref[i] += part[:, i * LANES : (i + 1) * LANES]


def grid_rows(moved, time_count, space_count, rows_tm, slots):
    slot_rows = round_up(slots, 16)
    width = round_up(slots, LANES)
    day_dev = DAYS // time_count
    depth = space_count * width
    rows_step = rows_tm // GRID_STEPS
    return pl.pallas_call(
        functools.partial(grid_kernel, (time_count, space_count, rows_tm, slot_rows, width)),
        grid=(GRID_STEPS,),
        in_specs=[pl.BlockSpec(moved.shape, lambda i: (0, 0, 0))],
        out_specs=[
            pl.BlockSpec((rows_step, DAYS, LANES), lambda i: (i, 0, 0)),
            pl.BlockSpec((DAYS // LANES, RANK, LANES), lambda i: (0, 0, 0)),
        ],
        out_shape=[
            jax.ShapeDtypeStruct((rows_tm, DAYS, LANES), jnp.bfloat16),
            jax.ShapeDtypeStruct((DAYS // LANES, RANK, LANES), jnp.float32),
        ],
        scratch_shapes=[
            pltpu.VMEM((time_count, depth, 2 * LANES), jnp.bfloat16),
            pltpu.VMEM((time_count, day_dev, depth), jnp.bfloat16),
            pltpu.VMEM((time_count, 8, depth), jnp.float32),
        ],
        compiler_params=pltpu.CompilerParams(vmem_limit_bytes=VMEM),
        name="grid_and_gram",
    )(moved)


def dot_f32(a, b, dims=(((1,), (0,)), ((), ()))):
    return lax.dot_general(a, b, dims, precision=lax.Precision.HIGHEST, preferred_element_type=jnp.float32)


def lower_inverse(a):
    n = a.shape[0]
    tiles = [a[8 * i : 8 * i + 8, :] for i in range(n // 8)]
    lane = lax.broadcasted_iota(jnp.int32, (8, n), 1)
    below = lax.broadcasted_iota(jnp.int32, (8, n), 0)
    lane_row = lax.broadcasted_iota(jnp.int32, (1, n), 1)
    for k in range(n):
        at, sub = divmod(k, 8)
        row = tiles[at][sub : sub + 1, :]
        scaled = jnp.where(lane_row == k, 1.0, row) * (1.0 / row[:, k : k + 1])
        for i in range(at, n // 8):
            col = jnp.broadcast_to(tiles[i][:, k : k + 1], (8, n))
            if i == at:
                col = jnp.where(below > sub, col, 0.0)
                base = jnp.where((lane == k) & (below > sub), 0.0, tiles[i])
            else:
                base = jnp.where(lane == k, 0.0, tiles[i])
            tiles[i] = base - col * scaled
    out = []
    for i, t in enumerate(tiles):
        diag = below + 8 * i
        pivot = jnp.sum(jnp.where(lane == diag, t, 0.0), axis=1, keepdims=True)
        out.append(jnp.where(lane < diag, t, jnp.where(lane == diag, 1.0, 0.0)) * lax.rsqrt(pivot))
    return jnp.concatenate(out, axis=0)


def solve_kernel(scale, gram_ref, basis_ref, prop_ref):
    h = LANES
    pieces = DAYS // h
    corner = gram_ref[1, :h, :]
    x1 = lower_inverse(gram_ref[0, :h, :])
    r12 = dot_f32(x1, corner)
    x2 = lower_inverse(gram_ref[1, h:, :] - dot_f32(r12, r12, FIRST_FIRST))
    mixed = -dot_f32(x2, dot_f32(r12, x1, FIRST_FIRST))
    lower = jnp.concatenate(
        [
            jnp.concatenate([x1, jnp.zeros((h, h), jnp.float32)], axis=1),
            jnp.concatenate([mixed, x2], axis=1),
        ],
        axis=0,
    )
    basis_ref[...] = (scale * lower).astype(jnp.bfloat16)

    down = lax.broadcasted_iota(jnp.int32, (RANK, DAYS), 0)
    across = lax.broadcasted_iota(jnp.int32, (RANK, DAYS), 1)
    gram = jnp.concatenate([gram_ref[i] for i in range(pieces)], axis=1)
    factor = jnp.where(across >= down, dot_f32(lower, gram), 0.0)
    ahead = jnp.where(across < DAYS - 1, pltpu.roll(factor, DAYS - 1, 1), 0.0)
    cross = dot_f32(ahead, factor, LAST_LAST)
    polar = cross / jnp.sqrt(jnp.sum(cross * cross) + 1e-06)
    for _ in range(ITERS):
        square = dot_f32(polar, polar, LAST_LAST)
        polar = 1.5 * polar - 0.5 * dot_f32(square, polar)
    prop_ref[...] = math.sqrt(RANK) * polar


def solve(gram, cell_total):
    return pl.pallas_call(
        functools.partial(solve_kernel, math.sqrt(cell_total)),
        out_shape=[
            jax.ShapeDtypeStruct((RANK, RANK), jnp.bfloat16),
            jax.ShapeDtypeStruct((RANK, RANK), jnp.float32),
        ],
        compiler_params=pltpu.CompilerParams(vmem_limit_bytes=VMEM),
        name="factor_and_polar",
    )(gram)


def body(pixels, weights, tile_index, tile_row, granule_day):
    swath_rows = pixels.shape[0]
    width = pixels.shape[1]
    space_count = lax.axis_size("space")
    time_count = lax.axis_size("tm")
    dest_count = time_count * space_count
    rows_tm = GR_DEV // time_count
    slots = 2 * swath_rows // space_count // time_count
    axes = ("tm", "space")
    packed = pack(pixels, weights, tile_index, tile_row, granule_day, time_count, space_count, rows_tm, slots)
    moved = lax.all_to_all(packed, axes, split_axis=0, concat_axis=0, tiled=True)
    field, partial_gram = grid_rows(moved, time_count, space_count, rows_tm, slots)
    pieces = partial_gram.reshape(dest_count, -1, LANES)
    pieces = lax.all_to_all(pieces, axes, split_axis=0, concat_axis=0, tiled=True)
    mine = jnp.sum(pieces, axis=0, keepdims=True)
    gram = lax.all_to_all(jnp.broadcast_to(mine, pieces.shape), axes, split_axis=0, concat_axis=0, tiled=True)
    cell_total = space_count * GR_DEV * width
    scaled_lower, propagator = solve(gram.reshape(partial_gram.shape), cell_total)
    basis = jnp.einsum("kd,rdp->rkp", scaled_lower, field[:, :RANK, :], preferred_element_type=jnp.float32)
    return (field[None], basis.astype(jnp.bfloat16)[None], propagator)


def solution(mesh):
    placed = (
        P(("tm", "space"), None),
        P(("tm", "space")),
        P(("tm", "space")),
        P(("tm", "space")),
        P(("tm", "space")),
    )
    return jax.shard_map(
        body,
        mesh=mesh,
        in_specs=placed,
        out_specs=(P("space", "tm", None, None), P("space", "tm", None, None), P()),
        check_vma=False,
    )
```

time: 535 us -> 195 us (0.36); the launches traced: 527 us -> 194 us
  other arithmetic: 198 us -> 0.05 us
  waiting for transfers between devices: 188 us -> 0 us
  blocking collectives: 0 us -> 109 us
  local copies, waits for them, and re-layouts: 81.9 us -> 2.61 us
  Pallas kernels: 0 us -> 79 us
  starting transfers between devices: 19.3 us -> 0 us
  matrix products: 20.8 us -> 2.64 us
  between operations: 18.2 us -> 0.66 us
    psum x1 -> x0, waiting for transfers between devices: 127 us -> none  [body(): gram = lax.psum(partial_gram, ('tm', 'space'))]
    another operation x20 -> x0, other arithmetic: 117 us -> none  [the longest x14 87.3 us: body(): lower = jnp.linalg.cholesky(gram)]
    all_to_all x0 -> x3, blocking collectives: none -> 109 us  [the longest x1 71.5 us: body(): lax.all_to_all(packed, axes, split_axis=0, concat_axis=0, tiled=True)]
    pallas_call x0 -> x3, Pallas kernels: none -> 79 us  [the longest x1 33.8 us: solve(): pl.pallas_call(functools.partial(solve_kernel, math.sqrt(cell_total)), ou...]
    scatter-add x1 -> x0, other arithmetic: 72.8 us -> none  [grid_rows(): jnp.zeros((cell_count, width), jnp.float32).at[target_buf.reshape(-1)]]
    scatter x3 -> x0, local copies, waits for them, and re-layouts: 70.6 us -> none  [the longest x1 35.8 us: pack_rows(): weight_buf = jnp.zeros((size,), weights.dtype).at[position].set(weights)]
    all_to_all x3 -> x0, waiting for transfers between devices: 60.7 us -> none  [the longest x1 60.7 us: body(): lax.all_to_all(packed[0], ('tm', 'space'), split_axis=0, concat_axis=0, t...]
    all_to_all x3 -> x0, starting transfers between devices: 19 us -> none  [the longest x1 7.3 us: body(): lax.all_to_all(packed[1], ('tm', 'space'), split_axis=0, concat_axis=0, t...]
  transfers between devices with their start and end apart: 4 -> 0, of which waited for: 2 -> 0; matrix products, arithmetic and copies ran while one was open for 7% -> 0% of each run, Pallas kernels for 0% -> 0%
where the time goes in v1:
time: 195 us; the launch traced here: 194 us
  blocking collectives  109 us (56%)
  Pallas kernels  79 us (41%)
  matrix products  2.64 us (1%)
  local copies, waits for them, and re-layouts  2.61 us (1%)
    all_to_all x1, blocking collectives, body(): lax.all_to_all(packed, axes, split_axis=0, concat_axis=0, tiled=True)  71.5 us
    pallas_call x1, Pallas kernels, solve(): pl.pallas_call(functools.partial(solve_kernel, math.sqrt(cell_total)), ou...  33.8 us
    pallas_call x1, Pallas kernels, grid_rows(): pl.pallas_call(functools.partial(grid_kernel, (time_count, space_count, r...  29 us
    all_to_all x1, blocking collectives, body(): lax.all_to_all(pieces, axes, split_axis=0, concat_axis=0, tiled=True)  19 us
    all_to_all x1, blocking collectives, body(): lax.all_to_all(jnp.broadcast_to(mine, pieces.shape), axes, split_axis=0,...  18.7 us
    pallas_call x1, Pallas kernels, pack(): pl.pallas_call(functools.partial(pack_kernel, (time_count, space_count, r...  16.2 us

profile of v1, /device:TPU:0, one launch (start us, length us, event | category | flops | bytes accessed | tf_op | source)
XLA Modules:
  0.0 194.1 jit_solution(14088995817660394360)
XLA Ops:
  0.6 16.2 %pack.1 = bf16[32,336,128]{2,1,0:T(8,128)(2,1)} custom-call(s32[40,128]{1,0:T(8,128)} %bitcast.17, s32[40,128]{1,0:T(8,128)} %bitcast.18, s32[40,128]{1,0:T(8,128)} %bitcast.19, bf16[40,128]{1,0:T(8,128)(2,1)} %bitcast.20, bf16[5120,128]{1,0:T(8,128)(2,1)} %pix_ref.1), custom_call_target="tpu_custom_call" | custom-call | tf_op jit(solution)/shard_map/pack/pallas_call | solution.py:110
  16.8 71.5 %all_to_all.15.moved_ref = bf16[32,336,128]{2,1,0:T(8,128)(2,1)} all-to-all(bf16[32,336,128]{2,1,0:T(8,128)(2,1)} %pack.1), channel_id=1, replica_groups=mesh['tm'=4,'space'=8] {'tm','space'}, dimensions={0} | all-to-all | bytes 5505024 | tf_op jit(solution)/shard_map/all_to_all | solution.py:301
  88.3 29.0 %grid_and_gram.1 = (bf16[40,512,128]{2,1,0:T(8,128)(2,1)}, f32[4,256,128]{2,1,0:T(8,128)}) custom-call(bf16[32,336,128]{2,1,0:T(8,128)(2,1)} %all_to_all.15.moved_ref), custom_call_target="tpu_custom_call" | custom-call | tf_op jit(solution)/shard_map/grid_and_gram/pallas_call | solution.py:197
  117.3 19.0 %all_to_all.16 = f32[32,32,128]{2,1,0:T(8,128)S(1)} all-to-all(f32[32,32,128]{2,1,0:T(8,128)} %bitcast.16), channel_id=1, replica_groups=mesh['tm'=4,'space'=8] {'tm','space'}, dimensions={0} | all-to-all | bytes 1048576 | tf_op jit(solution)/shard_map/all_to_all | solution.py:304
  136.3 0.1 broadcast_in_dim.13
  136.3 18.7 %all_to_all.17 = f32[32,32,128]{2,1,0:T(8,128)} all-to-all(f32[32,32,128]{2,1,0:T(8,128)S(1)} %broadcast_in_dim.13), channel_id=1, replica_groups=mesh['tm'=4,'space'=8] {'tm','space'}, dimensions={0} | all-to-all | bytes 1048576 | tf_op jit(solution)/shard_map/all_to_all | solution.py:306
  155.1 33.8 %factor_and_polar.1 = (bf16[256,256]{1,0:T(8,128)(2,1)}, f32[256,256]{1,0:T(8,128)}) custom-call(f32[4,256,128]{2,1,0:T(8,128)} %bitcast.14), custom_call_target="tpu_custom_call" | custom-call | tf_op jit(solution)/shard_map/factor_and_polar/pallas_call | solution.py:280
  188.9 2.6 %convert_bitcast_fusion = bf16[1,40,256,128]{2,3,1,0:T(8,128)(2,1)S(1)} fusion(bf16[40,512,128]{2,1,0:T(8,128)(2,1)} %get-tuple-element.7, bf16[256,256]{1,0:T(8,128)(2,1)} %get-tuple-element.9), kind=kOutput, calls=%fused_computation | convolution fusion | flops 672399360 | bytes 5373952 | tf_op jit(solution)/shard_map/kd,rdp->rkp/dot_general | solution.py:309
  191.6 2.6 %copy.9 = bf16[1,40,256,128]{3,2,1,0:T(8,128)(2,1)} copy(bf16[1,40,256,128]{2,3,1,0:T(8,128)(2,1)S(1)} %convert_bitcast_fusion) | data formatting | bytes 5242880
  (1 shorter events, 0.0 us)
